TPU v7x, 32 devices: a whole 2x2x4 slice. The times are simulated.
32 devices in a mesh: section: 4 (over y, x), dp: 8 (over z, core).
Axes of the slice: x: 2, y: 2, z: 4, core: 2. Of those that a mesh axis runs over, the one named last changes fastest.
Arguments:
- starting_learned_vectors: bfloat16 [256, 32, 768], P('dp'), may hold values from -6 to 6
- frozen_picture_vectors: bfloat16 [96, 257, 1408], P('dp'), may hold values from -6 to 6
- texts_per_picture: int32 [8, 12], P('dp'), may hold values from 1 to 5, 32 in all within a row
- early_triple_matrix: bfloat16 [768, 2304], replicated, may hold values from -0.21875 to 0.21875
- early_mixing_exit_matrix: bfloat16 [768, 768], replicated, may hold values from -0.4375 to 0.4375
- picture_asker_matrix: bfloat16 [768, 768], replicated, may hold values from -0.21875 to 0.21875
- picture_pair_matrix: bfloat16 [1408, 1536], replicated, may hold values from -0.15625 to 0.15625
- picture_exit_matrix: bfloat16 [768, 768], replicated, may hold values from -0.4375 to 0.4375
- early_widen_matrix: bfloat16 [768, 3072], replicated, may hold values from -0.21875 to 0.21875
- early_narrow_matrix: bfloat16 [3072, 768], replicated, may hold values from -0.109375 to 0.109375
- later_triple_matrix: bfloat16 [768, 2304], replicated, may hold values from -0.21875 to 0.21875
- later_mixing_exit_matrix: bfloat16 [768, 768], replicated, may hold values from -0.4375 to 0.4375
- later_widen_matrix: bfloat16 [768, 3072], replicated, may hold values from -0.21875 to 0.21875
- later_narrow_matrix: bfloat16 [3072, 768], replicated, may hold values from -0.109375 to 0.109375
- standardizer_factors: float32 [5, 768], replicated, may hold values from 0.5 to 1.5
- picture_divisors: float32 [12], replicated, may hold values from 0.45 to 2.8
- closing_cotangent: bfloat16 [256, 32, 768], P('dp'), may hold values from -6 to 6
Outputs:
- final_states: float32 [256, 32, 768], P('dp', None, 'section')
- query_grad: float32 [256, 32, 768], P('dp', None, 'section')
- first_project_grad: float32 [768, 2304], P('dp', 'section')
- first_output_grad: float32 [768, 768], P('dp', 'section')
- image_query_grad: float32 [768, 768], P('dp', 'section')
- image_keyval_grad: float32 [1408, 1536], P('dp', 'section')
- image_output_grad: float32 [768, 768], P('dp', 'section')
- first_expand_grad: float32 [768, 3072], P('dp', 'section')
- first_reduce_grad: float32 [3072, 768], P('dp', 'section')
- second_project_grad: float32 [768, 2304], P('dp', 'section')
- second_output_grad: float32 [768, 768], P('dp', 'section')
- second_expand_grad: float32 [768, 3072], P('dp', 'section')
- second_reduce_grad: float32 [3072, 768], P('dp', 'section')
- norm_gains_grad: float32 [5, 768], replicated
- temperature_grad: float32 [12], replicated
Inputs may be any that keep to these rules, and one draw needn't show every extreme that they name: `texts_per_picture`: row d holds the caption counts of the 12 images of index d of dp, in the order of their items, and sums to 32; every row has an image with 5 captions.
All inputs are finite; a program needn't handle non-finite values.
Results may differ from a plain program's by a relative error of at most 0.035.
The roundings to bfloat16 on the way count: a program that leaves them out, or rounds other values in their place, can miss the bound.
Values may be sent and summed in bfloat16 or wider, within the bound.
A program may use at most 832 MiB of HBM per device.

v0:
```python
import math

import jax
import jax.numpy as jnp
from jax import lax
from jax.sharding import PartitionSpec as P

MICRO = 4


EPSILON = 1e-06


def passed_along(value, axis, by):
    size = lax.axis_size(axis)
    pairs = [(i, i + by) for i in range(size) if 0 <= i + by < size]
    return lax.ppermute(value, axis, pairs)


def as_sent(value):

    def short(part):
        return part.astype(jnp.bfloat16) if part.dtype == jnp.float32 else part

    return jax.tree.map(short, value)


def broadcast(value, axis, source):
    kept = jnp.where(lax.axis_index(axis) == source, value, 0).astype(value.dtype)
    return lax.psum(kept, axis)


def matmul(left_side, right_side):
    return jnp.dot(left_side, right_side, preferred_element_type=jnp.float32)


def matmul_left(left_side, right_side):
    return lax.dot_general(
        left_side, right_side, (((0,), (0,)), ((), ())), preferred_element_type=jnp.float32
    )


def matmul_right(left_side, right_side):
    return lax.dot_general(
        left_side, right_side, (((1,), (1,)), ((), ())), preferred_element_type=jnp.float32
    )


def gelu_exact(values):
    return jax.nn.gelu(values, approximate=False)


def layer_norm(summed_in, standardizer_factor):
    mean_row = jnp.mean(summed_in, axis=-1, keepdims=True)
    centred = summed_in - mean_row
    spread = jnp.mean(centred * centred, axis=-1, keepdims=True)
    inverse = lax.rsqrt(spread + EPSILON)
    normed = centred * inverse
    return (normed * standardizer_factor, (normed, inverse))


def norm_back(grad_out, standardizer_factor, norm_saved):
    normed, inverse = norm_saved
    grad_normed = grad_out * standardizer_factor
    grad_gain = jnp.sum(grad_out * normed, axis=0)
    grad_summed = inverse * (
        grad_normed
        - jnp.mean(grad_normed, axis=-1, keepdims=True)
        - normed * jnp.mean(grad_normed * normed, axis=-1, keepdims=True)
    )
    return (grad_summed, grad_gain)


def attend_self(
    entries_given, w_project, exit_matrix, standardizer_factor, query_count, focus_unit_number
):
    row_count, model_width = entries_given.shape
    head_size = model_width // focus_unit_number
    item_count = row_count // query_count
    lowered = entries_given.astype(jnp.bfloat16)
    joined = (
        matmul(lowered, w_project)
        .astype(jnp.bfloat16)
        .reshape(item_count, query_count, 3, focus_unit_number, head_size)
    )
    queries, key_part, value_part = (joined[:, :, 0], joined[:, :, 1], joined[:, :, 2])
    raw_scores = jnp.einsum(
        "iqhd,ikhd->ihqk", queries, key_part, preferred_element_type=jnp.float32
    )
    multiplier = 1.0 / math.sqrt(head_size)
    softened = jax.nn.softmax(raw_scores * multiplier, axis=-1)
    soft_low = softened.astype(jnp.bfloat16)
    mixed_heads = (
        jnp.einsum("ihqk,ikhd->iqhd", soft_low, value_part, preferred_element_type=jnp.float32)
        .astype(jnp.bfloat16)
        .reshape(row_count, model_width)
    )
    branch = matmul(mixed_heads, exit_matrix)
    result, norm_saved = layer_norm(entries_given + branch, standardizer_factor)
    return (result, (lowered, joined, softened, soft_low, mixed_heads, norm_saved))


def attend_self_back(
    grad_out, w_project, exit_matrix, standardizer_factor, saved_all, query_count, focus_unit_number
):
    lowered, joined, softened, soft_low, mixed_heads, norm_saved = saved_all
    row_count, model_width = mixed_heads.shape
    head_size = model_width // focus_unit_number
    item_count = row_count // query_count
    queries, key_part, value_part = (joined[:, :, 0], joined[:, :, 1], joined[:, :, 2])
    multiplier = 1.0 / math.sqrt(head_size)
    grad_summed, grad_gain = norm_back(grad_out, standardizer_factor, norm_saved)
    grad_branch = grad_summed.astype(jnp.bfloat16)
    grad_w_output = matmul_left(mixed_heads, grad_branch)
    grad_mixed = (
        matmul_right(grad_branch, exit_matrix)
        .astype(jnp.bfloat16)
        .reshape(item_count, query_count, focus_unit_number, head_size)
    )
    grad_soft = jnp.einsum(
        "iqhd,ikhd->ihqk", grad_mixed, value_part, preferred_element_type=jnp.float32
    )
    grad_value = jnp.einsum(
        "ihqk,iqhd->ikhd", soft_low, grad_mixed, preferred_element_type=jnp.float32
    )
    grad_scores = softened * (grad_soft - jnp.sum(softened * grad_soft, axis=-1, keepdims=True))
    grad_raw = (grad_scores * multiplier).astype(jnp.bfloat16)
    grad_query = jnp.einsum(
        "ihqk,ikhd->iqhd", grad_raw, key_part, preferred_element_type=jnp.float32
    )
    grad_key = jnp.einsum("ihqk,iqhd->ikhd", grad_raw, queries, preferred_element_type=jnp.float32)
    grad_joined = (
        jnp.stack([grad_query, grad_key, grad_value], axis=2)
        .astype(jnp.bfloat16)
        .reshape(row_count, 3 * model_width)
    )
    grad_w_project = matmul_left(lowered, grad_joined)
    grad_inputs = grad_summed + matmul_right(grad_joined, w_project)
    return (grad_inputs, grad_gain, grad_w_project, grad_w_output)


def attend_image(
    entries_given,
    paired_entries,
    asker_matrix,
    exit_matrix,
    standardizer_factor,
    exponent_divisor,
    query_count,
    focus_unit_number,
):
    row_count, model_width = entries_given.shape
    head_size = model_width // focus_unit_number
    item_count = row_count // query_count
    patches = paired_entries.shape[1]
    lowered = entries_given.astype(jnp.bfloat16)
    queries = (
        matmul(lowered, asker_matrix)
        .astype(jnp.bfloat16)
        .reshape(item_count, query_count, focus_unit_number, head_size)
    )
    keyval_pairs = paired_entries.reshape(item_count, patches, 2, focus_unit_number, head_size)
    key_part, value_part = (keyval_pairs[:, :, 0], keyval_pairs[:, :, 1])
    raw_scores = jnp.einsum(
        "iqhd,iphd->ihqp", queries, key_part, preferred_element_type=jnp.float32
    )
    clamped_amounts = jnp.clip(exponent_divisor, 0.5, 2.0)
    multiplier = 1.0 / math.sqrt(head_size) / clamped_amounts
    softened = jax.nn.softmax(raw_scores * multiplier[None, :, None, None], axis=-1)
    soft_low = softened.astype(jnp.bfloat16)
    mixed_heads = (
        jnp.einsum("ihqp,iphd->iqhd", soft_low, value_part, preferred_element_type=jnp.float32)
        .astype(jnp.bfloat16)
        .reshape(row_count, model_width)
    )
    branch = matmul(mixed_heads, exit_matrix)
    result, norm_saved = layer_norm(entries_given + branch, standardizer_factor)
    return (
        result,
        (
            lowered,
            queries,
            key_part,
            value_part,
            raw_scores,
            multiplier,
            clamped_amounts,
            softened,
            soft_low,
            mixed_heads,
            norm_saved,
        ),
    )


def attend_image_back(
    grad_out,
    asker_matrix,
    exit_matrix,
    standardizer_factor,
    exponent_divisor,
    saved_all,
    query_count,
    focus_unit_number,
):
    (
        lowered,
        queries,
        key_part,
        value_part,
        raw_scores,
        multiplier,
        clamped_amounts,
        softened,
        soft_low,
        mixed_heads,
        norm_saved,
    ) = saved_all
    row_count, model_width = mixed_heads.shape
    head_size = model_width // focus_unit_number
    item_count = row_count // query_count
    patches = key_part.shape[1]
    grad_summed, grad_gain = norm_back(grad_out, standardizer_factor, norm_saved)
    grad_branch = grad_summed.astype(jnp.bfloat16)
    grad_w_output = matmul_left(mixed_heads, grad_branch)
    grad_mixed = (
        matmul_right(grad_branch, exit_matrix)
        .astype(jnp.bfloat16)
        .reshape(item_count, query_count, focus_unit_number, head_size)
    )
    grad_soft = jnp.einsum(
        "iqhd,iphd->ihqp", grad_mixed, value_part, preferred_element_type=jnp.float32
    )
    grad_value = jnp.einsum(
        "ihqp,iqhd->iphd", soft_low, grad_mixed, preferred_element_type=jnp.float32
    )
    grad_scores = softened * (grad_soft - jnp.sum(softened * grad_soft, axis=-1, keepdims=True))
    grad_scaling = jnp.sum(grad_scores * raw_scores, axis=(0, 2, 3))
    interior_result = ((exponent_divisor > 0.5) & (exponent_divisor < 2.0)).astype(jnp.float32)
    grad_temper = grad_scaling * (-multiplier / clamped_amounts) * interior_result
    grad_raw = (grad_scores * multiplier[None, :, None, None]).astype(jnp.bfloat16)
    grad_query = (
        jnp.einsum("ihqp,iphd->iqhd", grad_raw, key_part, preferred_element_type=jnp.float32)
        .astype(jnp.bfloat16)
        .reshape(row_count, model_width)
    )
    grad_key = jnp.einsum("ihqp,iqhd->iphd", grad_raw, queries, preferred_element_type=jnp.float32)
    grad_keyval = jnp.stack([grad_key, grad_value], axis=2).reshape(
        item_count, patches, 2 * model_width
    )
    grad_w_query = matmul_left(lowered, grad_query)
    grad_inputs = grad_summed + matmul_right(grad_query, asker_matrix)
    return (grad_inputs, grad_gain, grad_w_query, grad_w_output, grad_temper, grad_keyval)


def feed_forward(entries_given, w_expand, w_reduce, standardizer_factor):
    lowered = entries_given.astype(jnp.bfloat16)
    hidden = matmul(lowered, w_expand).astype(jnp.bfloat16)
    active = gelu_exact(hidden.astype(jnp.float32)).astype(jnp.bfloat16)
    branch = matmul(active, w_reduce)
    result, norm_saved = layer_norm(entries_given + branch, standardizer_factor)
    return (result, (lowered, hidden, active, norm_saved))


def feed_forward_back(grad_out, w_expand, w_reduce, standardizer_factor, saved_all):
    lowered, hidden, active, norm_saved = saved_all
    grad_summed, grad_gain = norm_back(grad_out, standardizer_factor, norm_saved)
    grad_branch = grad_summed.astype(jnp.bfloat16)
    grad_w_reduce = matmul_left(active, grad_branch)
    grad_active = matmul_right(grad_branch, w_reduce)
    pullback = jax.vjp(gelu_exact, hidden.astype(jnp.float32))[1]
    grad_hidden = pullback(grad_active)[0].astype(jnp.bfloat16)
    grad_w_expand = matmul_left(lowered, grad_hidden)
    grad_inputs = grad_summed + matmul_right(grad_hidden, w_expand)
    return (grad_inputs, grad_gain, grad_w_expand, grad_w_reduce)


def body(
    starting_learned_vectors,
    frozen_picture_vectors,
    texts_per_picture,
    early_triple_matrix,
    early_mixing_exit_matrix,
    picture_asker_matrix,
    picture_pair_matrix,
    picture_exit_matrix,
    early_widen_matrix,
    early_narrow_matrix,
    later_triple_matrix,
    later_mixing_exit_matrix,
    later_widen_matrix,
    later_narrow_matrix,
    standardizer_factors,
    picture_divisors,
    closing_cotangent,
):
    sections = lax.axis_size("section")
    section_index = lax.axis_index("section")
    last_section = sections - 1
    item_count, query_count, model_width = starting_learned_vectors.shape
    focus_unit_number = picture_divisors.shape[0]
    images, patches, feat_width = frozen_picture_vectors.shape
    hidden_width = early_widen_matrix.shape[1]
    batches = MICRO
    per_batch = item_count // batches
    row_count = per_batch * query_count
    tick_count = batches + sections - 1
    flat_length = max(6 * model_width * model_width, 2 * model_width * hidden_width)
    count_ends = jnp.cumsum(texts_per_picture[0])
    positions = jnp.arange(item_count, dtype=jnp.int32)
    image_of = jnp.sum((count_ends[None, :] <= positions[:, None]).astype(jnp.int32), axis=1)
    image_ids = jnp.arange(images, dtype=jnp.int32)

    def project(feat_block):
        count_rows = feat_block.shape[0]
        flattened = matmul(
            feat_block.reshape(count_rows * patches, feat_width), picture_pair_matrix
        )
        return flattened.astype(jnp.bfloat16).reshape(count_rows, patches, 2 * model_width)

    def no_keyval(feat_block):
        return jnp.zeros((images, patches, 2 * model_width), jnp.bfloat16)

    paired_matrix = lax.cond(section_index == 0, project, no_keyval, frozen_picture_vectors)

    def batch_images(batch_index):
        return lax.dynamic_slice_in_dim(image_of, batch_index * per_batch, per_batch, 0)

    def section_zero(entries_given, batch_index):
        hidden_between, first_saved = attend_self(
            entries_given,
            early_triple_matrix,
            early_mixing_exit_matrix,
            standardizer_factors[0],
            query_count,
            focus_unit_number,
        )
        chosen = jnp.take(paired_matrix, batch_images(batch_index), axis=0)
        result, second_saved = attend_image(
            hidden_between,
            chosen,
            picture_asker_matrix,
            picture_exit_matrix,
            standardizer_factors[1],
            picture_divisors,
            query_count,
            focus_unit_number,
        )
        return (result, (first_saved, second_saved))

    def section_one(entries_given, batch_index):
        return feed_forward(
            entries_given, early_widen_matrix, early_narrow_matrix, standardizer_factors[2]
        )

    def section_two(entries_given):
        return attend_self(
            entries_given,
            later_triple_matrix,
            later_mixing_exit_matrix,
            standardizer_factors[3],
            query_count,
            focus_unit_number,
        )

    def section_three(entries_given, batch_index):
        return feed_forward(
            entries_given, later_widen_matrix, later_narrow_matrix, standardizer_factors[4]
        )

    def forward_zero(entries_given, batch_index):
        return section_zero(entries_given, batch_index)[0]

    def forward_one(entries_given, batch_index):
        return section_one(entries_given, batch_index)[0]

    def forward_two(entries_given, batch_index):
        return section_two(entries_given)[0]

    def forward_three(entries_given, batch_index):
        return section_three(entries_given, batch_index)[0]

    def forward_spare(entries_given, batch_index):
        return entries_given

    forward_branches = [forward_zero, forward_one, forward_two, forward_three, forward_spare]
    batches_in = starting_learned_vectors.reshape(batches, row_count, model_width)
    kept = jnp.zeros((batches, row_count, model_width), jnp.float32)
    finals = jnp.zeros((batches, row_count, model_width), jnp.float32)
    arriving = jnp.zeros((row_count, model_width), jnp.float32)
    for moment in range(tick_count):
        batch_index = moment - section_index
        active_now = (batch_index >= 0) & (batch_index < batches)
        clipped = jnp.clip(batch_index, 0, batches - 1)
        loaded = batches_in[min(moment, batches - 1)].astype(jnp.float32)
        entries_given = jnp.where(section_index == 0, loaded, arriving)
        branch_pick = jnp.where(active_now, section_index, sections)
        result = lax.switch(branch_pick, forward_branches, entries_given, clipped)
        kept = lax.dynamic_update_index_in_dim(
            kept, jnp.where(active_now, entries_given, kept[clipped]), clipped, 0
        )
        finals = lax.dynamic_update_index_in_dim(
            finals,
            jnp.where(active_now & (section_index == last_section), result, finals[clipped]),
            clipped,
            0,
        )
        if moment + 1 < tick_count:
            arriving = passed_along(result, "section", 1)

    def pack_terms(term_list):
        joined_flat = jnp.concatenate([term_value.reshape(-1) for term_value in term_list])
        return jnp.pad(joined_flat, (0, flat_length - joined_flat.shape[0]))

    empty_keyval = jnp.zeros((per_batch, patches, 2 * model_width), jnp.float32)
    empty_gains = jnp.zeros(standardizer_factors.shape, jnp.float32)
    empty_temper = jnp.zeros(picture_divisors.shape, jnp.float32)

    def back_zero(grad_out, batch_index):
        entries_given = kept[batch_index]
        hidden_between, first_saved = attend_self(
            entries_given,
            early_triple_matrix,
            early_mixing_exit_matrix,
            standardizer_factors[0],
            query_count,
            focus_unit_number,
        )
        chosen = jnp.take(paired_matrix, batch_images(batch_index), axis=0)
        result, second_saved = attend_image(
            hidden_between,
            chosen,
            picture_asker_matrix,
            picture_exit_matrix,
            standardizer_factors[1],
            picture_divisors,
            query_count,
            focus_unit_number,
        )
        grad_middle, gain_image, grad_query_w, grad_output_w, grad_temper, grad_keyval = (
            attend_image_back(
                grad_out,
                picture_asker_matrix,
                picture_exit_matrix,
                standardizer_factors[1],
                picture_divisors,
                second_saved,
                query_count,
                focus_unit_number,
            )
        )
        grad_inputs, gain_self, grad_project_w, grad_self_out = attend_self_back(
            grad_middle,
            early_triple_matrix,
            early_mixing_exit_matrix,
            standardizer_factors[0],
            first_saved,
            query_count,
            focus_unit_number,
        )
        flat_terms = pack_terms([grad_project_w, grad_self_out, grad_query_w, grad_output_w])
        gain_terms = empty_gains.at[0].set(gain_self).at[1].set(gain_image)
        return (grad_inputs, flat_terms, gain_terms, grad_temper, grad_keyval)

    def back_hidden(saved_section, w_expand, w_reduce, gain_row):

        def back_fn(grad_out, batch_index):
            result, saved_all = saved_section(kept[batch_index], batch_index)
            grad_inputs, grad_gain, grad_w_expand, grad_w_reduce = feed_forward_back(
                grad_out, w_expand, w_reduce, standardizer_factors[gain_row], saved_all
            )
            return (
                grad_inputs,
                pack_terms([grad_w_expand, grad_w_reduce]),
                empty_gains.at[gain_row].set(grad_gain),
                empty_temper,
                empty_keyval,
            )

        return back_fn

    def back_two(grad_out, batch_index):
        result, saved_all = section_two(kept[batch_index])
        grad_inputs, grad_gain, grad_project_w, grad_self_out = attend_self_back(
            grad_out,
            later_triple_matrix,
            later_mixing_exit_matrix,
            standardizer_factors[3],
            saved_all,
            query_count,
            focus_unit_number,
        )
        return (
            grad_inputs,
            pack_terms([grad_project_w, grad_self_out]),
            empty_gains.at[3].set(grad_gain),
            empty_temper,
            empty_keyval,
        )

    def back_spare(grad_out, batch_index):
        return (
            jnp.zeros_like(grad_out),
            jnp.zeros((flat_length,), jnp.float32),
            empty_gains,
            empty_temper,
            empty_keyval,
        )

    backward_branches = [
        back_zero,
        back_hidden(section_one, early_widen_matrix, early_narrow_matrix, 2),
        back_two,
        back_hidden(section_three, later_widen_matrix, later_narrow_matrix, 4),
        back_spare,
    ]
    grads_in = closing_cotangent.reshape(batches, row_count, model_width)
    input_grads = jnp.zeros((batches, row_count, model_width), jnp.float32)
    arriving_grad = jnp.zeros((row_count, model_width), jnp.float32)
    packed_total = jnp.zeros((flat_length,), jnp.float32)
    gains_total = empty_gains
    temper_total = empty_temper
    keyval_total = jnp.zeros((images, patches, 2 * model_width), jnp.float32)
    for moment in range(tick_count):
        batch_index = moment - (last_section - section_index)
        active_now = (batch_index >= 0) & (batch_index < batches)
        clipped = jnp.clip(batch_index, 0, batches - 1)
        loaded = grads_in[min(moment, batches - 1)].astype(jnp.float32)
        incoming = jnp.where(section_index == last_section, loaded, arriving_grad)
        branch_pick = jnp.where(active_now, section_index, sections)
        result, flat_term, gain_term, temper_term, keyval_term = lax.switch(
            branch_pick, backward_branches, incoming, clipped
        )
        packed_total = packed_total + flat_term
        gains_total = gains_total + gain_term
        temper_total = temper_total + temper_term
        onehot = (batch_images(clipped)[:, None] == image_ids[None, :]).astype(jnp.float32)
        keyval_total = keyval_total + jnp.einsum(
            "bj,bpc->jpc", onehot, keyval_term, precision=lax.Precision.HIGHEST
        )
        input_grads = lax.dynamic_update_index_in_dim(
            input_grads,
            jnp.where(active_now & (section_index == 0), result, input_grads[clipped]),
            clipped,
            0,
        )
        if moment + 1 < tick_count:
            arriving_grad = passed_along(result, "section", -1)

    def unpack_flat(shapes):
        pieces_out = []
        offset = 0
        for row_total, col_total in shapes:
            pieces_out.append(
                packed_total[offset : offset + row_total * col_total].reshape(row_total, col_total)
            )
            offset = offset + row_total * col_total
        return pieces_out

    attend_layout = unpack_flat(
        [
            (model_width, 3 * model_width),
            (model_width, model_width),
            (model_width, model_width),
            (model_width, model_width),
        ]
    )
    hidden_layout = unpack_flat([(model_width, hidden_width), (hidden_width, model_width)])
    keyval_low = keyval_total.astype(jnp.bfloat16)

    def owner_grad():
        return matmul_left(
            frozen_picture_vectors.reshape(images * patches, feat_width),
            keyval_low.reshape(images * patches, 2 * model_width),
        )

    def other_grad():
        return jnp.zeros((feat_width, 2 * model_width), jnp.float32)

    keyval_weight_grad = lax.cond(section_index == 0, owner_grad, other_grad)

    def keep_if(term_value, owner):
        return jnp.where(section_index == owner, term_value, jnp.zeros_like(term_value))

    pieces = (
        lax.psum_scatter(
            keep_if(attend_layout[0], 0).astype(jnp.bfloat16), "dp", scatter_dimension=0, tiled=True
        ).astype(jnp.float32),
        lax.psum_scatter(
            keep_if(attend_layout[1], 0).astype(jnp.bfloat16), "dp", scatter_dimension=0, tiled=True
        ).astype(jnp.float32),
        lax.psum_scatter(
            keep_if(attend_layout[2], 0).astype(jnp.bfloat16), "dp", scatter_dimension=0, tiled=True
        ).astype(jnp.float32),
        lax.psum_scatter(
            keyval_weight_grad.astype(jnp.bfloat16), "dp", scatter_dimension=0, tiled=True
        ).astype(jnp.float32),
        lax.psum_scatter(
            keep_if(attend_layout[3], 0).astype(jnp.bfloat16), "dp", scatter_dimension=0, tiled=True
        ).astype(jnp.float32),
        lax.psum_scatter(
            keep_if(hidden_layout[0], 1).astype(jnp.bfloat16), "dp", scatter_dimension=0, tiled=True
        ).astype(jnp.float32),
        lax.psum_scatter(
            keep_if(hidden_layout[1], 1).astype(jnp.bfloat16), "dp", scatter_dimension=0, tiled=True
        ).astype(jnp.float32),
        lax.psum_scatter(
            keep_if(attend_layout[0], 2).astype(jnp.bfloat16), "dp", scatter_dimension=0, tiled=True
        ).astype(jnp.float32),
        lax.psum_scatter(
            keep_if(attend_layout[1], 2).astype(jnp.bfloat16), "dp", scatter_dimension=0, tiled=True
        ).astype(jnp.float32),
        lax.psum_scatter(
            keep_if(hidden_layout[0], 3).astype(jnp.bfloat16), "dp", scatter_dimension=0, tiled=True
        ).astype(jnp.float32),
        lax.psum_scatter(
            keep_if(hidden_layout[1], 3).astype(jnp.bfloat16), "dp", scatter_dimension=0, tiled=True
        ).astype(jnp.float32),
    )
    placed = jax.tree.map(
        lambda part: part.astype(jnp.float32),
        lax.psum_scatter(as_sent(tuple(pieces)), "section", scatter_dimension=1, tiled=True),
    )
    small_sums = lax.psum((gains_total, temper_total), ("section", "dp"))
    share_width = model_width // sections
    homed_states = (
        broadcast(finals.astype(jnp.bfloat16), "section", last_section)
        .astype(finals.dtype)
        .reshape(item_count, query_count, model_width)
    )
    final_part = lax.dynamic_slice_in_dim(homed_states, section_index * share_width, share_width, 2)
    homed_grads = (
        broadcast(input_grads.astype(jnp.bfloat16), "section", 0)
        .astype(input_grads.dtype)
        .reshape(item_count, query_count, model_width)
    )
    grad_part = lax.dynamic_slice_in_dim(homed_grads, section_index * share_width, share_width, 2)
    return (final_part, grad_part) + tuple(placed) + (small_sums[0], small_sums[1])


def solution(mesh):
    return jax.shard_map(
        body,
        mesh=mesh,
        in_specs=(
            P("dp", None, None),
            P("dp", None, None),
            P("dp", None),
            P(),
            P(),
            P(),
            P(),
            P(),
            P(),
            P(),
            P(),
            P(),
            P(),
            P(),
            P(),
            P(),
            P("dp", None, None),
        ),
        out_specs=(
            P("dp", None, "section"),
            P("dp", None, "section"),
            P("dp", "section"),
            P("dp", "section"),
            P("dp", "section"),
            P("dp", "section"),
            P("dp", "section"),
            P("dp", "section"),
            P("dp", "section"),
            P("dp", "section"),
            P("dp", "section"),
            P("dp", "section"),
            P("dp", "section"),
            P(),
            P(),
        ),
        check_vma=False,
    )
```

profile of v0, /device:TPU:0, one launch (start us, length us, event | category | flops | bytes accessed | tf_op | source)
XLA Modules:
  0.0 3034.6 jit_solution(15435620164320075975)
XLA Ops:
  10.7 43.3 %conditional.16 = (bf16[12,257,1536]{2,1,0:T(8,128)(2,1)}) conditional(s32[]{:T(128)} %convert_element_type.1793, () %tuple.406, (bf16[12,257,1408]{2,1,0:T(8,128)(2,1)}, bf16[1408,1536]{1,0:T(8,128)(2,1)}) %tuple.407), branch_computations={%region_2.3_spmd, %region_3.4_spmd} | conditional | flops 13344196608 | bytes 58801160 | solution.py:324
  54.1 86.2 %conditional.17 = (f32[256,768]{1,0:T(8,128)}) conditional(s32[]{:T(128)} %clamp.56, (f32[256,768]{1,0:T(8,128)S(1)}, bf16[768,2304]{1,0:T(8,128)(2,1)}, bf16[768,768]{1,0:T(8,128)(2,1)S(1)}, f32[5,768]{1,0:T(8,128)S(1)}, s32[]{:T(128)}, /*index=5*/s32[32]{0:T(128)}, bf16[12,257,1536]{2,1,0:T(8,128)(2,1)}, ...), branch_computations={%region_4.14_spmd, %region_13.17_spmd, %region_16.22_spmd, %region... | conditional | flops 2470379776 | bytes 130094592 | solution.py:398
  160.7 92.3 %conditional.18 = (f32[256,768]{1,0:T(8,128)}) conditional(s32[]{:T(128)} %clamp.57, (f32[256,768]{1,0:T(8,128)}, bf16[768,2304]{1,0:T(8,128)(2,1)}, bf16[768,768]{1,0:T(8,128)(2,1)}, f32[5,768]{1,0:T(8,128)S(1)}, s32[]{:T(128)}, /*index=5*/s32[32]{0:T(128)}, bf16[12,257,1536]{2,1,0:T(8,128)(2,1)}, ...), branch_computations={%region_25.35_spmd, %region_34.38_spmd, %region_37.43_spmd, %regio... | conditional | flops 2470379776 | bytes 127604192 | solution.py:398
  273.8 90.3 %conditional.19 = (f32[256,768]{1,0:T(8,128)}) conditional(s32[]{:T(128)} %clamp.58, (f32[256,768]{1,0:T(8,128)}, bf16[768,2304]{1,0:T(8,128)(2,1)}, bf16[768,768]{1,0:T(8,128)(2,1)}, f32[5,768]{1,0:T(8,128)S(1)}, s32[]{:T(128)}, /*index=5*/s32[32]{0:T(128)}, bf16[12,257,1536]{2,1,0:T(8,128)(2,1)}, ...), branch_computations={%region_46.0_spmd, %region_55.59_spmd, %region_58.64_spmd, %region... | conditional | flops 2470379776 | bytes 127604624 | solution.py:398
  383.3 93.3 %conditional.20 = (f32[256,768]{1,0:T(8,128)}) conditional(s32[]{:T(128)} %clamp.59, (f32[256,768]{1,0:T(8,128)}, bf16[768,2304]{1,0:T(8,128)(2,1)}, bf16[768,768]{1,0:T(8,128)(2,1)}, f32[5,768]{1,0:T(8,128)}, s32[]{:T(128)}, /*index=5*/s32[32]{0:T(128)}, bf16[12,257,1536]{2,1,0:T(8,128)(2,1)}, ...), branch_computations={%region_67.0_spmd, %region_76.80_spmd, %region_79.85_spmd, %region... | conditional | flops 2470379776 | bytes 127604400 | solution.py:398
  590.4 39.2 %conditional.24 = (f32[256,768]{1,0:T(8,128)}, f32[4718592]{0:T(1024)}, f32[5,768]{1,0:T(8,128)S(1)}, f32[12]{0:T(128)S(1)}, f32[8,257,1536]{2,0,1:T(8,128)}) conditional(s32[]{:T(128)} %clamp.63, (s32[]{:T(128)}, f32[4,256,768]{2,1,0:T(8,128)S(1)}, bf16[768,2304]{1,0:T(8,128)(2,1)}, bf16[768,768]{1,0:T(8,128)(2,1)}, ...), branch_computations={%region_152.171_spmd, %region_170.177_spmd, %region_176.0_spmd, %r... | conditional | flops 7325416960 | bytes 463423712 | solution.py:531
  633.2 35.0 %collective-permute-done.6 = f32[256,768]{1,0:T(8,128)} collective-permute-done((f32[256,768]{1,0:T(8,128)}, f32[256,768]{1,0:T(8,128)}, u32[]{:S(2)}, u32[]{:S(2)}) %collective-permute-start.6) | collective-permute-done | bytes 786464 | tf_op jit(solution)/shard_map/ppermute | solution.py:17
  670.2 39.3 %conditional.25 = (f32[256,768]{1,0:T(8,128)}, f32[4718592]{0:T(1024)}, f32[5,768]{1,0:T(8,128)S(1)}, f32[12]{0:T(128)S(1)}, f32[8,257,1536]{2,0,1:T(8,128)}) conditional(s32[]{:T(128)} %clamp.64, (s32[]{:T(128)}, f32[4,256,768]{2,1,0:T(8,128)S(1)}, bf16[768,2304]{1,0:T(8,128)(2,1)}, bf16[768,768]{1,0:T(8,128)(2,1)}, ...), branch_computations={%region_192.211_spmd, %region_210.217_spmd, %region_216.226_spmd, ... | conditional | flops 7325416960 | bytes 463423712 | solution.py:531
  730.8 40.0 %conditional.26 = (f32[256,768]{1,0:T(8,128)}, f32[4718592]{0:T(1024)}, f32[5,768]{1,0:T(8,128)}, f32[12]{0:T(128)S(1)}, f32[8,257,1536]{2,0,1:T(8,128)}) conditional(s32[]{:T(128)} %clamp.65, (s32[]{:T(128)}, f32[4,256,768]{2,1,0:T(8,128)S(1)}, bf16[768,2304]{1,0:T(8,128)(2,1)}, bf16[768,768]{1,0:T(8,128)(2,1)}, ...), branch_computations={%region_232.251_spmd, %region_250.257_spmd, %region_256.266_spmd, ... | conditional | flops 7325416960 | bytes 463325088 | solution.py:531
  772.2 192.5 %collective-permute-done.8 = f32[256,768]{1,0:T(8,128)} collective-permute-done((f32[256,768]{1,0:T(8,128)}, f32[256,768]{1,0:T(8,128)}, u32[]{:S(2)}, u32[]{:S(2)}) %collective-permute-start.8) | collective-permute-done | bytes 786464 | tf_op jit(solution)/shard_map/ppermute | solution.py:17
  966.8 267.8 %conditional.27 = (f32[256,768]{1,0:T(8,128)}, f32[4718592]{0:T(1024)}, f32[5,768]{1,0:T(8,128)}, f32[12]{0:T(128)S(1)}, f32[8,257,1536]{2,0,1:T(8,128)}) conditional(s32[]{:T(128)} %clamp.66, (s32[]{:T(128)}, f32[4,256,768]{2,1,0:T(8,128)S(1)}, bf16[768,2304]{1,0:T(8,128)(2,1)}, bf16[768,768]{1,0:T(8,128)(2,1)}, ...), branch_computations={%region_272.291_spmd, %region_290.297_spmd, %region_296.306_spmd, ... | conditional | flops 7325416960 | bytes 463325088 | solution.py:531
  1253.3 267.8 %conditional.28 = (f32[256,768]{1,0:T(8,128)}, f32[4718592]{0:T(1024)}, f32[5,768]{1,0:T(8,128)}, f32[12]{0:T(128)S(1)}, f32[8,257,1536]{2,0,1:T(8,128)}) conditional(s32[]{:T(128)} %clamp.67, (s32[]{:T(128)}, f32[4,256,768]{2,1,0:T(8,128)S(1)}, bf16[768,2304]{1,0:T(8,128)(2,1)}, bf16[768,768]{1,0:T(8,128)(2,1)}, ...), branch_computations={%region_312.331_spmd, %region_330.337_spmd, %region_336.346_spmd, ... | conditional | flops 7325416960 | bytes 463325088 | solution.py:531
  1538.8 267.7 %conditional.29 = (f32[256,768]{1,0:T(8,128)}, f32[4718592]{0:T(1024)}, f32[5,768]{1,0:T(8,128)}, f32[12]{0:T(128)S(1)}, f32[8,257,1536]{2,0,1:T(8,128)}) conditional(s32[]{:T(128)} %clamp.68, (s32[]{:T(128)}, f32[4,256,768]{2,1,0:T(8,128)S(1)}, bf16[768,2304]{1,0:T(8,128)(2,1)}, bf16[768,768]{1,0:T(8,128)(2,1)}, ...), branch_computations={%region_352.0_spmd, %region_370.377_spmd, %region_376.386_spmd, %r... | conditional | flops 7325416960 | bytes 463325088 | solution.py:531
  1823.3 263.0 %conditional.30 = (f32[256,768]{1,0:T(8,128)}, f32[4718592]{0:T(1024)}, f32[5,768]{1,0:T(8,128)S(1)}, f32[12]{0:T(128)S(1)}, f32[8,257,1536]{2,0,1:T(8,128)}) conditional(s32[]{:T(128)} %clamp.69, (s32[]{:T(128)}, f32[4,256,768]{2,1,0:T(8,128)S(1)}, bf16[768,2304]{1,0:T(8,128)(2,1)}, bf16[768,768]{1,0:T(8,128)(2,1)}, ...), branch_computations={%region_392.411_spmd, %region_410.417_spmd, %region_416.426_spmd, ... | conditional | flops 7325416960 | bytes 472860960 | solution.py:531
  2086.3 44.0 %add_add_fusion = bf16[4718592]{0:T(1024)(128)(2,1)} fusion(f32[4718592]{0:T(1024)} %get-tuple-element.1622, f32[4718592]{0:T(1024)} %get-tuple-element.1621, f32[4718592]{0:T(1024)} %get-tuple-element.1620, f32[4718592]{0:T(1024)} %get-tuple-element.1619, f32[4718592]{0:T(1024)} %get-tuple-element.1618, f32[4718592]{0:T(1024)} %get-tuple-element.1616, ...), kind=kLoop, calls=%fused_computation.4058 | loop fusion | flops 33030144 | bytes 141557760 | tf_op jit(solution)/shard_map/add | solution.py:534
  2261.4 57.0 %add_convert_fusion = bf16[12,257,1536]{2,0,1:T(8,128)(2,1)} fusion(f32[12,257,1536]{2,0,1:T(8,128)} %fusion.2928, f32[12,257,1536]{2,0,1:T(8,128)} %fusion.2925, f32[12,257,1536]{2,0,1:T(8,128)} %fusion.2922, f32[12,257,1536]{2,0,1:T(8,128)} %fusion.2919, f32[12,257,1536]{2,0,1:T(8,128)} %fusion.2913, f32[12,257,1536]{2,0,1:T(8,128)} %fusion.2916, ...), kind=kOutput, calls=%fused_computation.4057 | convolution fusion | flops 487913568 | bytes 135794720 | tf_op jit(solution)/shard_map/bj,bpc->jpc/dot_general | solution.py:538
  2433.2 29.6 reduce-scatter.55.cloned.1.call-done
  2465.0 53.5 %reduce-scatter.65.cloned.1.call-done = bf16[384,768]{1,0:T(8,128)(2,1)} async-done(((bf16[3072,768]{1,0:T(8,128)(2,1)}), bf16[384,768]{1,0:T(8,128)(2,1)}) %reduce-scatter.65.cloned.1.call-update) | async-done | bytes 589840 | tf_op jit(solution)/shard_map/reduce_scatter | solution.py:616
  2520.9 53.3 %reduce-scatter.51.cloned.1.call-done = bf16[96,3072]{1,0:T(8,128)(2,1)} async-done(((bf16[768,3072]{1,0:T(8,128)(2,1)}), bf16[96,3072]{1,0:T(8,128)(2,1)}) %reduce-scatter.51.cloned.1.call-update) | async-done | bytes 589840 | tf_op jit(solution)/shard_map/reduce_scatter | solution.py:601
  2574.3 55.7 %reduce-scatter.61.cloned.1.call-done = bf16[96,3072]{1,0:T(8,128)(2,1)} async-done(((bf16[768,3072]{1,0:T(8,128)(2,1)}), bf16[96,3072]{1,0:T(8,128)(2,1)}) %reduce-scatter.61.cloned.1.call-update) | async-done | bytes 589840 | tf_op jit(solution)/shard_map/reduce_scatter | solution.py:613
  2630.2 38.5 %all-reduce.42 = (f32[5,768]{1,0:T(8,128)}, f32[12]{0:T(128)}) all-reduce(f32[5,768]{1,0:T(8,128)S(1)} %add_add_fusion.1, f32[12]{0:T(128)S(1)} %add_add_fusion.2), channel_id=1, replica_groups=mesh['section'=4,'dp'=8] {'section','dp'}, use_global_device_ids=true, to_apply=%region_457.459 | all-reduce | flops 3852 | bytes 30816 | tf_op jit(solution)/shard_map/psum | solution.py:624
  2739.7 89.1 %all-reduce.46.cloned.1.call-done = (bf16[32,32,768]{2,1,0:T(8,128)(2,1)}, bf16[32,32,768]{2,1,0:T(8,128)(2,1)}) async-done(((bf16[32,32,768]{2,1,0:T(8,128)(2,1)}, bf16[32,32,768]{2,1,0:T(8,128)(2,1)}), (bf16[32,32,768]{2,1,0:T(8,128)(2,1)}, bf16[32,32,768]{2,1,0:T(8,128)(2,1)})) %all-reduce.46.cloned.1.call-update) | async-done | bytes 3145744 | tf_op jit(solution)/shard_map/psum | solution.py:30
  2886.4 27.3 reduce-scatter.73.cloned.1.call-done
  2999.3 26.6 reduce-scatter.63.cloned.1.call-done
  (1061 shorter events, 2086.8 us)
Async XLA Ops:
  7.2 2406.6 %reduce-scatter.43.cloned.1.call-start = ((), (), s32[]{:S(2)}) async-start(), calls=%async_computation.23 | async-start | bytes 1327104 | tf_op jit(solution)/shard_map/reduce_scatter | solution.py:589
  770.9 193.8 %collective-permute-start.8 = (f32[256,768]{1,0:T(8,128)}, f32[256,768]{1,0:T(8,128)}, u32[]{:S(2)}, u32[]{:S(2)}) collective-permute-start(f32[256,768]{1,0:T(8,128)} %get-tuple-element.1611), channel_id=1, source_target_pairs={{8,0},{16,8},{24,16},{9,1},{17,9},{25,17},{10,2},{18,10},{26,18},{... | collective-permute-start | bytes 2359304 | tf_op jit(solution)/shard_map/ppermute | solution.py:17
  2137.8 279.1 %reduce-scatter.45.cloned.1.call-start = ((), (), s32[]{:S(2)}) async-start(), calls=%async_computation.24 | async-start | bytes 1327104 | tf_op jit(solution)/shard_map/reduce_scatter | solution.py:592
  2141.2 278.8 %reduce-scatter.49.cloned.1.call-start = ((), (), s32[]{:S(2)}) async-start(), calls=%async_computation.26 | async-start | bytes 1327104 | tf_op jit(solution)/shard_map/reduce_scatter | solution.py:598
  2143.1 280.0 %reduce-scatter.59.cloned.1.call-start = ((), (), s32[]{:S(2)}) async-start(), calls=%async_computation.31 | async-start | bytes 1327104 | tf_op jit(solution)/shard_map/reduce_scatter | solution.py:610
  2145.1 281.3 %reduce-scatter.41.cloned.1.call-start = ((), (), s32[]{:S(2)}) async-start(), calls=%async_computation.22 | async-start | bytes 3981312 | tf_op jit(solution)/shard_map/reduce_scatter | solution.py:586
  2157.6 271.0 %reduce-scatter.57.cloned.1.call-start = ((), (), s32[]{:S(2)}) async-start(), calls=%async_computation.30 | async-start | bytes 3981312 | tf_op jit(solution)/shard_map/reduce_scatter | solution.py:607
  2243.6 187.4 %reduce-scatter.47.cloned.1.call-start = ((), (), s32[]{:S(2)}) async-start(), calls=%async_computation.25 | async-start | bytes 4866048 | tf_op jit(solution)/shard_map/reduce_scatter | solution.py:595
  2342.9 119.9 %reduce-scatter.55.cloned.1.call-start = ((), (), s32[]{:S(2)}) async-start(), calls=%async_computation.29 | async-start | bytes 5308416 | tf_op jit(solution)/shard_map/reduce_scatter | solution.py:604
  2363.5 155.1 %reduce-scatter.65.cloned.1.call-start = ((), (), s32[]{:S(2)}) async-start(), calls=%async_computation.34 | async-start | bytes 5308416 | tf_op jit(solution)/shard_map/reduce_scatter | solution.py:616
  2372.9 201.3 %reduce-scatter.51.cloned.1.call-start = ((), (), s32[]{:S(2)}) async-start(), calls=%async_computation.27 | async-start | bytes 5308416 | tf_op jit(solution)/shard_map/reduce_scatter | solution.py:601
  2381.2 248.7 %reduce-scatter.61.cloned.1.call-start = ((), (), s32[]{:S(2)}) async-start(), calls=%async_computation.32 | async-start | bytes 5308416 | tf_op jit(solution)/shard_map/reduce_scatter | solution.py:613
  2389.6 279.0 %reduce-scatter.69.cloned.1.call-start = ((), (), s32[]{:S(2)}) async-start(), calls=%async_computation.36 | async-start | bytes 245760
  2415.5 267.8 %reduce-scatter.71.cloned.1.call-start = ((), (), s32[]{:S(2)}) async-start(), calls=%async_computation.37 | async-start | bytes 245760
  2418.7 292.1 %reduce-scatter.75.cloned.1.call-start = ((), (), s32[]{:S(2)}) async-start(), calls=%async_computation.39 | async-start | bytes 245760
  2421.8 316.3 %reduce-scatter.81.cloned.1.call-start = ((), (), s32[]{:S(2)}) async-start(), calls=%async_computation.42 | async-start | bytes 245760
  2424.9 403.9 %all-reduce.46.cloned.1.call-start = ((), (), s32[]{:S(2)}) async-start(), calls=%async_computation.44 | async-start | bytes 6291456 | tf_op jit(solution)/shard_map/psum | solution.py:30
  2426.3 430.3 %reduce-scatter.67.cloned.1.call-start = ((), (), s32[]{:S(2)}) async-start(), calls=%async_computation.35 | async-start | bytes 737280
  2428.5 456.2 %reduce-scatter.79.cloned.1.call-start = ((), (), s32[]{:S(2)}) async-start(), calls=%async_computation.41 | async-start | bytes 737280
  2430.8 482.9 %reduce-scatter.73.cloned.1.call-start = ((), (), s32[]{:S(2)}) async-start(), calls=%async_computation.38 | async-start | bytes 983040
  2433.2 508.4 %reduce-scatter.77.cloned.1.call-start = ((), (), s32[]{:S(2)}) async-start(), calls=%async_computation.40 | async-start | bytes 737280
  2465.0 504.7 %reduce-scatter.83.cloned.1.call-start = ((), (), s32[]{:S(2)}) async-start(), calls=%async_computation.43 | async-start | bytes 737280
  2520.8 476.9 %reduce-scatter.53.cloned.1.call-start = ((), (), s32[]{:S(2)}) async-start(), calls=%async_computation.28 | async-start | bytes 737280 | tf_op jit(solution)/shard_map/reduce_scatter | solution.py:622
  2574.2 451.7 %reduce-scatter.63.cloned.1.call-start = ((), (), s32[]{:S(2)}) async-start(), calls=%async_computation.33 | async-start | bytes 737280 | tf_op jit(solution)/shard_map/reduce_scatter | solution.py:622
  (221 other events, 6078.2 us)
Sparse Core Ops, SparseCore 0:
  2137.9 28.5 reduce-scatter.42
  2168.8 30.8 reduce-scatter.44
  2202.0 31.2 reduce-scatter.48
  2235.4 30.8 reduce-scatter.58
  2268.5 42.0 reduce-scatter.40
  2312.8 42.2 reduce-scatter.56
  2357.5 49.7 reduce-scatter.46
  2409.7 53.0 reduce-scatter.54
  2465.2 53.3 reduce-scatter.64
  2520.8 53.3 reduce-scatter.50
  2576.6 53.3 reduce-scatter.60
  2633.4 22.3 reduce-scatter.68
  2659.3 23.9 reduce-scatter.70
  2686.7 23.9 reduce-scatter.74
  2714.1 23.9 reduce-scatter.80
  2741.4 87.3 all-reduce.45
  2831.5 25.0 reduce-scatter.66
  2859.6 25.0 reduce-scatter.78
  2887.6 26.0 reduce-scatter.72
  2916.4 25.0 reduce-scatter.76
  2944.6 25.0 reduce-scatter.82
  2972.6 25.0 reduce-scatter.52
  3000.8 25.0 reduce-scatter.62
where the time goes:
time: 3050 us; the launch traced here: 3030 us
  waiting for transfers between devices  889 us (29%)
  local copies, waits for them, and re-layouts  731 us (24%)
  matrix products  593 us (19%)
  other arithmetic  417 us (14%)
  loops' own time  311 us (10%)
  starting transfers between devices  40.1 us (1%)
  blocking collectives  38.5 us (1%)
    ppermute x12, waiting for transfers between devices, passed_along(): return lax.ppermute(value, axis, pairs)  360 us
    unnamed x32, waiting for transfers between devices  194 us
    another operation x7, loops' own time, body(): lax.switch(branch_pick, backward_branches, incoming, clipped)  179 us
    dot_general x7, matrix products, body(): jnp.einsum('bj,bpc->jpc', onehot, keyval_term, precision=lax.Precision.HI...  152 us
    another operation x7, loops' own time, body(): result = lax.switch(branch_pick, forward_branches, entries_given, clipped)  132 us
    dot_general x33, matrix products, matmul(): return jnp.dot(left_side, right_side, preferred_element_type=jnp.float32)  102 us
    psum x1, waiting for transfers between devices, broadcast(): return lax.psum(kept, axis)  89.1 us
    sub x4, other arithmetic, attend_image_back(): grad_soft - jnp.sum(softened * grad_soft, axis=-1, keepdims=True)  84 us
  transfers between devices with their start and end apart: 35, of which 27 were waited for; matrix products, arithmetic and copies ran while one was open for 11% of the time, Pallas kernels for 0%

commit v1 on v0

v1 whole, which is shorter than its diff:
```python
import math

import jax
import jax.numpy as jnp
from jax import lax
from jax.sharding import PartitionSpec as P

EPSILON = 1e-06
BF = jnp.bfloat16
F32 = jnp.float32


def mm(left, right):
    return jnp.dot(left, right, preferred_element_type=F32)


def mm_tn(left, right):
    return lax.dot_general(left, right, (((0,), (0,)), ((), ())), preferred_element_type=F32)


def mm_nt(left, right):
    return lax.dot_general(left, right, (((1,), (1,)), ((), ())), preferred_element_type=F32)


def layer_norm(z, gain):
    centred = z - jnp.mean(z, axis=-1, keepdims=True)
    inverse = lax.rsqrt(jnp.mean(centred * centred, axis=-1, keepdims=True) + EPSILON)
    normed = centred * inverse
    return normed * gain, normed, inverse


def norm_back(dout, gain, normed, inverse):
    dn = dout * gain
    dgain = jnp.sum(dout * normed, axis=0)
    dz = inverse * (
        dn
        - jnp.mean(dn, axis=-1, keepdims=True)
        - normed * jnp.mean(dn * normed, axis=-1, keepdims=True)
    )
    return dz, dgain


def gelu(u):
    return u * (1.0 + lax.erf(u * (0.5**0.5))) * 0.5


def gelu_slope(u):
    return 0.5 * (1.0 + lax.erf(u * (0.5**0.5))) + u * jnp.exp(-0.5 * u * u) * (
        1.0 / math.sqrt(2.0 * math.pi)
    )


def swap(value, axis, bit):
    size = lax.axis_size(axis)
    return lax.ppermute(value, axis, [(i, i ^ bit) for i in range(size)])


def pick(value, index, axis):
    return lax.dynamic_index_in_dim(value, index, axis, keepdims=False)


def add_low(left, right):
    return (left.astype(F32) + right.astype(F32)).astype(BF)


def section_blocks(value):
    rows, width = value.shape
    parts = lax.axis_size("section")
    return value.reshape(rows, parts, width // parts).transpose(1, 0, 2)


def exchange(blocks):
    me = lax.axis_index("section")
    parts = lax.axis_size("section")
    out = blocks
    for bit in range(1, parts):
        got = swap(pick(blocks, me ^ bit, 0), "section", bit)
        out = lax.dynamic_update_index_in_dim(out, got, me ^ bit, 0)
    return out


def cols_to_section(value):
    return exchange(section_blocks(value))


def rows_from_section(blocks):
    got = exchange(blocks)
    parts, rows, width = got.shape
    return got.transpose(1, 0, 2).reshape(rows, parts * width)


def line_sum(blocks):
    n = blocks.shape[0]
    p = lax.axis_index("dp") // 2
    size = lax.axis_size("dp")
    kept = blocks
    for k in range(n - 1):
        up_at = jnp.clip(n - 1 - k + p, 0, n - 1)
        down_at = jnp.clip(p - (n - 1 - k), 0, n - 1)
        up_pairs = [(2 * q + c, 2 * q + 2 + c) for q in range(min(k, n - 2) + 1) for c in (0, 1)]
        down_pairs = [
            (2 * q + c, 2 * q - 2 + c) for q in range(max(n - 1 - k, 1), n) for c in (0, 1)
        ]
        up = lax.ppermute(pick(kept, up_at, 0), "dp", up_pairs)
        down = lax.ppermute(pick(kept, down_at, 0), "dp", down_pairs)
        up_to = jnp.clip(n - 2 - k + p, 0, n - 1)
        down_to = jnp.clip(p + 1 - (n - 1 - k), 0, n - 1)
        kept = lax.dynamic_update_index_in_dim(kept, add_low(pick(kept, up_to, 0), up), up_to, 0)
        kept = lax.dynamic_update_index_in_dim(
            kept, add_low(pick(kept, down_to, 0), down), down_to, 0
        )
    del size
    return pick(kept, p, 0)


def core_sum(unit):
    parts, dp, r, w = unit.shape
    c = lax.axis_index("dp") % 2
    pairs = unit.reshape(parts, dp // 2, 2, r, w)
    return add_low(pick(pairs, c, 2), swap(pick(pairs, 1 - c, 2), "dp", 1))


def plane_sum(unit):
    parts, n, r, w = unit.shape
    me = lax.axis_index("section")
    low, high = me % 2, me // 2
    square = unit.reshape(2, 2, n, r, w)
    a, b = square[:, :, :, : r // 2], square[:, :, :, r // 2 :]
    a = add_low(pick(a, low, 1), swap(pick(a, 1 - low, 1), "section", 1))
    b = add_low(pick(b, high, 0), swap(pick(b, 1 - high, 0), "section", 2))
    a = add_low(pick(a, high, 0), swap(pick(a, 1 - high, 0), "section", 2))
    b = add_low(pick(b, low, 0), swap(pick(b, 1 - low, 0), "section", 1))
    return jnp.concatenate([a, b], axis=1)


def home(unit):
    return line_sum(plane_sum(core_sum(unit)))


def unit_of(grad, dp, sections):
    rows, cols = grad.shape
    return (
        grad.astype(BF)
        .reshape(dp, rows // dp, sections, cols // sections)
        .transpose(2, 0, 1, 3)
    )


def all_sum(value):
    for axis in ("dp", "section"):
        bit = 1
        while bit < lax.axis_size(axis):
            value = value + swap(value, axis, bit)
            bit *= 2
    return value


def self_parts(joined, items, query_count, heads):
    rows = joined.shape[0]
    width = joined.shape[1] // 3
    parts = joined.reshape(items, query_count, 3, heads, width // heads)
    return parts[:, :, 0], parts[:, :, 1], parts[:, :, 2]


def self_forward(x, w_project, w_exit, gain, query_count, heads):
    rows, width = x.shape
    items = rows // query_count
    low = x.astype(BF)
    joined = mm(low, w_project).astype(BF)
    q, k, v = self_parts(joined, items, query_count, heads)
    scale = 1.0 / math.sqrt(width // heads)
    t = jnp.einsum("iqhd,ikhd->ihqk", q, k, preferred_element_type=F32)
    p = jax.nn.softmax(t * scale, axis=-1)
    mixed = (
        jnp.einsum("ihqk,ikhd->iqhd", p.astype(BF), v, preferred_element_type=F32)
        .astype(BF)
        .reshape(rows, width)
    )
    out, normed, inverse = layer_norm(x + mm(mixed, w_exit), gain)
    return out, (low, joined, p, mixed, normed, inverse)


def self_backward(dout, w_project, w_exit, gain, saved, query_count, heads):
    low, joined, p, mixed, normed, inverse = saved
    rows, width = mixed.shape
    items = rows // query_count
    q, k, v = self_parts(joined, items, query_count, heads)
    scale = 1.0 / math.sqrt(width // heads)
    dz, dgain = norm_back(dout, gain, normed, inverse)
    da = dz.astype(BF)
    d_exit = mm_tn(mixed, da)
    do = mm_nt(da, w_exit).astype(BF).reshape(items, query_count, heads, width // heads)
    dp = jnp.einsum("iqhd,ikhd->ihqk", do, v, preferred_element_type=F32)
    dv = jnp.einsum("ihqk,iqhd->ikhd", p.astype(BF), do, preferred_element_type=F32)
    ds = p * (dp - jnp.sum(p * dp, axis=-1, keepdims=True))
    dt = (ds * scale).astype(BF)
    dq = jnp.einsum("ihqk,ikhd->iqhd", dt, k, preferred_element_type=F32)
    dk = jnp.einsum("ihqk,iqhd->ikhd", dt, q, preferred_element_type=F32)
    djoined = jnp.stack([dq, dk, dv], axis=2).astype(BF).reshape(rows, 3 * width)
    d_project = mm_tn(low, djoined)
    return dz + mm_nt(djoined, w_project), dgain, d_project, d_exit


def hidden_forward(x, w_expand, w_reduce, gain):
    low = x.astype(BF)
    u = mm(low, w_expand).astype(BF)
    m = gelu(u.astype(F32)).astype(BF)
    out, normed, inverse = layer_norm(x + mm(m, w_reduce), gain)
    return out, (low, u, m, normed, inverse)


def hidden_backward(dout, w_expand, w_reduce, gain, saved):
    low, u, m, normed, inverse = saved
    dz, dgain = norm_back(dout, gain, normed, inverse)
    da = dz.astype(BF)
    d_reduce = mm_tn(m, da)
    du = (mm_nt(da, w_reduce) * gelu_slope(u.astype(F32))).astype(BF)
    d_expand = mm_tn(low, du)
    return dz + mm_nt(du, w_expand), dgain, d_expand, d_reduce


def body(
    starting_learned_vectors,
    frozen_picture_vectors,
    texts_per_picture,
    early_triple_matrix,
    early_mixing_exit_matrix,
    picture_asker_matrix,
    picture_pair_matrix,
    picture_exit_matrix,
    early_widen_matrix,
    early_narrow_matrix,
    later_triple_matrix,
    later_mixing_exit_matrix,
    later_widen_matrix,
    later_narrow_matrix,
    standardizer_factors,
    picture_divisors,
    closing_cotangent,
):
    sections = lax.axis_size("section")
    dp = lax.axis_size("dp")
    me = lax.axis_index("section")
    item_count, query_count, width = starting_learned_vectors.shape
    heads = picture_divisors.shape[0]
    images, patches, feat = frozen_picture_vectors.shape
    own_items = item_count // sections
    rows = own_items * query_count
    own_heads = heads // sections
    head_size = width // heads
    own_width = width // sections
    gains = standardizer_factors

    ends = jnp.cumsum(texts_per_picture[0])
    positions = jnp.arange(item_count, dtype=jnp.int32)
    image_of = jnp.sum((ends[None, :] <= positions[:, None]).astype(jnp.int32), axis=1)
    onehot = (image_of[:, None] == jnp.arange(images)[None, :]).astype(F32)

    def own_rows(value):
        part = lax.dynamic_slice_in_dim(value, me * own_items, own_items, 0)
        return part.reshape(rows, width).astype(F32)

    w_pair = jnp.concatenate(
        [
            lax.dynamic_slice_in_dim(picture_pair_matrix, me * own_width, own_width, 1),
            lax.dynamic_slice_in_dim(picture_pair_matrix, width + me * own_width, own_width, 1),
        ],
        axis=1,
    )
    keyval = jnp.einsum(
        "npf,fc->npc", frozen_picture_vectors, w_pair, preferred_element_type=F32
    ).astype(BF)

    x0 = own_rows(starting_learned_vectors)
    h1, saved_self1 = self_forward(
        x0, early_triple_matrix, early_mixing_exit_matrix, gains[0], query_count, heads
    )
    low1 = h1.astype(BF)
    q_cols = cols_to_section(mm(low1, picture_asker_matrix).astype(BF))
    q = q_cols.reshape(item_count, query_count, own_heads, head_size)
    chosen = jnp.take(keyval, image_of, axis=0).reshape(
        item_count, patches, 2, own_heads, head_size
    )
    k, v = chosen[:, :, 0], chosen[:, :, 1]
    clamped = jnp.clip(picture_divisors, 0.5, 2.0)
    scale_all = 1.0 / math.sqrt(head_size) / clamped
    scale = lax.dynamic_slice_in_dim(scale_all, me * own_heads, own_heads, 0)
    t = jnp.einsum("iqhd,iphd->ihqp", q, k, preferred_element_type=F32)
    p = jax.nn.softmax(t * scale[None, :, None, None], axis=-1)
    p_low = p.astype(BF)
    o = jnp.einsum("ihqp,iphd->iqhd", p_low, v, preferred_element_type=F32).astype(BF)
    mixed = rows_from_section(o.reshape(sections, rows, own_width))
    h2, normed2, inverse2 = layer_norm(h1 + mm(mixed, picture_exit_matrix), gains[1])

    h3, saved_ff1 = hidden_forward(h2, early_widen_matrix, early_narrow_matrix, gains[2])
    h4, saved_self2 = self_forward(
        h3, later_triple_matrix, later_mixing_exit_matrix, gains[3], query_count, heads
    )
    h5, saved_ff2 = hidden_forward(h4, later_widen_matrix, later_narrow_matrix, gains[4])
    final_part = cols_to_section(h5.astype(BF)).astype(F32)
    final_part = final_part.reshape(item_count, query_count, own_width)

    def unit(grad):
        return unit_of(grad, dp, sections)

    def fold(blocks):
        parts, n, r, w = blocks.shape
        return blocks.reshape(parts, n, 4, r // 4, w).transpose(0, 1, 3, 2, 4).reshape(
            parts, n, r // 4, 4 * w
        )

    def unfold(block):
        r, w = block.shape
        return block.reshape(r, 4, w // 4).transpose(1, 0, 2).reshape(4 * r, w // 4)

    dout = own_rows(closing_cotangent)
    d5, dg4, d_expand2, d_reduce2 = hidden_backward(
        dout, later_widen_matrix, later_narrow_matrix, gains[4], saved_ff2
    )
    expand2 = home(unit(d_expand2))
    reduce2 = unfold(home(fold(unit(d_reduce2))))
    d4, dg3, d_project2, d_out2 = self_backward(
        d5, later_triple_matrix, later_mixing_exit_matrix, gains[3], saved_self2, query_count, heads
    )
    self2 = home(jnp.concatenate([unit(d_project2), unit(d_out2)], axis=3))
    d3, dg2, d_expand1, d_reduce1 = hidden_backward(
        d4, early_widen_matrix, early_narrow_matrix, gains[2], saved_ff1
    )
    expand1 = home(unit(d_expand1))
    reduce1 = unfold(home(fold(unit(d_reduce1))))

    dz2, dg1 = norm_back(d3, gains[1], normed2, inverse2)
    da2 = dz2.astype(BF)
    d_exit = mm_tn(mixed, da2)
    do = cols_to_section(mm_nt(da2, picture_exit_matrix).astype(BF))
    do = do.reshape(item_count, query_count, own_heads, head_size)
    dpr = jnp.einsum("iqhd,iphd->ihqp", do, v, preferred_element_type=F32)
    dv = jnp.einsum("ihqp,iqhd->iphd", p_low, do, preferred_element_type=F32)
    ds = p * (dpr - jnp.sum(p * dpr, axis=-1, keepdims=True))
    d_temper = jnp.sum(ds * t, axis=(0, 2, 3))
    dt = (ds * scale[None, :, None, None]).astype(BF)
    dq = jnp.einsum("ihqp,iphd->iqhd", dt, k, preferred_element_type=F32).astype(BF)
    dk = jnp.einsum("ihqp,iqhd->iphd", dt, q, preferred_element_type=F32)
    dkv = jnp.stack([dk, dv], axis=2).reshape(item_count, patches, 2 * own_width)
    dkv = jnp.einsum("bj,bpc->jpc", onehot, dkv, precision=lax.Precision.HIGHEST).astype(BF)
    d_pair = jnp.einsum("npf,npc->fc", frozen_picture_vectors, dkv, preferred_element_type=F32)
    pair_block = line_sum(
        core_sum(d_pair.astype(BF).reshape(1, dp, feat // dp, 2 * own_width))[0]
    )
    dq_rows = rows_from_section(dq.reshape(sections, rows, own_width))
    d_asker = mm_tn(low1, dq_rows)
    d2 = dz2 + mm_nt(dq_rows, picture_asker_matrix)
    image_units = home(jnp.concatenate([unit(d_asker), unit(d_exit)], axis=3))

    d1, dg0, d_project1, d_out1 = self_backward(
        d2, early_triple_matrix, early_mixing_exit_matrix, gains[0], saved_self1, query_count, heads
    )
    self1 = home(jnp.concatenate([unit(d_project1), unit(d_out1)], axis=3))
    grad_part = cols_to_section(d1.astype(BF)).astype(F32)
    grad_part = grad_part.reshape(item_count, query_count, own_width)

    pair_rows = pair_block.shape[0]
    half = sections // 2
    pair_halves = pair_block.reshape(pair_rows, 2, own_width).transpose(1, 0, 2)
    key_home, val_home = me // 2, half + me // 2
    sent = jnp.zeros((sections, pair_rows, own_width), BF)
    sent = lax.dynamic_update_index_in_dim(sent, pair_halves[0], key_home, 0)
    sent = lax.dynamic_update_index_in_dim(sent, pair_halves[1], val_home, 0)
    got = exchange(sent)
    first = (me % half) * 2
    pair_part = lax.dynamic_slice_in_dim(got, first, 2, 0)
    pair_part = pair_part.transpose(1, 0, 2).reshape(pair_rows, 2 * own_width).astype(F32)

    interior = ((picture_divisors > 0.5) & (picture_divisors < 2.0)).astype(F32)
    spread = jnp.zeros((heads,), F32)
    spread = lax.dynamic_update_slice_in_dim(spread, d_temper, me * own_heads, 0)
    spread = spread * (-scale_all / clamped) * interior
    small = jnp.concatenate([jnp.stack([dg0, dg1, dg2, dg3, dg4]).reshape(-1), spread])
    small = all_sum(small)
    gains_grad = small[: 5 * width].reshape(5, width)
    temper_grad = small[5 * width :]

    def f(block):
        return block.astype(F32)

    third = 3 * own_width
    return (
        final_part,
        grad_part,
        f(self1[:, :third]),
        f(self1[:, third:]),
        f(image_units[:, :own_width]),
        pair_part,
        f(image_units[:, own_width:]),
        f(expand1),
        f(reduce1),
        f(self2[:, :third]),
        f(self2[:, third:]),
        f(expand2),
        f(reduce2),
        gains_grad,
        temper_grad,
    )


def solution(mesh):
    return jax.shard_map(
        body,
        mesh=mesh,
        in_specs=(P("dp", None, None), P("dp", None, None), P("dp", None))
        + (P(),) * 13
        + (P("dp", None, None),),
        out_specs=(P("dp", None, "section"),) * 2 + (P("dp", "section"),) * 11 + (P(), P()),
        check_vma=False,
    )
```

time: 3050 us -> 1010 us (0.33)
  waiting for transfers between devices: 889 us -> 153 us
  matrix products: 593 us -> 162 us
  local copies, waits for them, and re-layouts: 731 us -> 346 us
  loops' own time: 311 us -> 0 us
  other arithmetic: 417 us -> 107 us
  starting transfers between devices: 40.1 us -> 220 us
  blocking collectives: 38.5 us -> 0 us
    dot_general x129 -> x49, matrix products: 562 us -> 153 us  [the longest x10 25.8 us: mm(): return jnp.dot(left, right, preferred_element_type=F32)]
    another operation x16 -> x0, loops' own time: 311 us -> none  [the longest x7 179 us: body(): lax.switch(branch_pick, backward_branches, incoming, clipped)]
    reduce_scatter x13 -> x0, waiting for transfers between devices: 245 us -> none  [the longest x1 55.7 us: body(): lax.psum_scatter(keep_if(hidden_layout[0], 3).astype(jnp.bfloat16), 'dp',...]
    ppermute x12 -> x110, waiting for transfers between devices: 360 us -> 153 us  [the longest x62 122 us: swap(): return lax.ppermute(value, axis, [(i, i ^ bit) for i in range(size)])]
    unnamed x32 -> x0, waiting for transfers between devices: 194 us -> none
    ppermute x12 -> x110, starting transfers between devices: 38.9 us -> 220 us  [the longest x62 102 us: swap(): return lax.ppermute(value, axis, [(i, i ^ bit) for i in range(size)])]
    sub x12 -> x2, other arithmetic: 120 us -> 25.4 us  [the longest x1 23.7 us: body(): ds = p * (dpr - jnp.sum(p * dpr, axis=-1, keepdims=True))]
    select_n x8 -> x0, local copies, waits for them, and re-layouts: 89.5 us -> none  [the longest x4 44.8 us: section_zero(): chosen = jnp.take(paired_matrix, batch_images(batch_index), axis=0)]
  transfers between devices with their start and end apart: 35 -> 110, of which waited for: 27 -> 44; matrix products, arithmetic and copies ran while one was open for 11% -> 44% of each run, Pallas kernels for 0% -> 0%
where the time goes in v1:
time: 1010 us; the launch traced here: 993 us
  local copies, waits for them, and re-layouts  346 us (34%)
  starting transfers between devices  220 us (22%)
  matrix products  162 us (16%)
  waiting for transfers between devices  153 us (15%)
  other arithmetic  107 us (11%)
    ppermute x62, waiting for transfers between devices, swap(): return lax.ppermute(value, axis, [(i, i ^ bit) for i in range(size)])  122 us
    ppermute x62, starting transfers between devices, swap(): return lax.ppermute(value, axis, [(i, i ^ bit) for i in range(size)])  102 us
    ppermute x24, starting transfers between devices, line_sum(): up = lax.ppermute(pick(kept, up_at, 0), 'dp', up_pairs)  96.4 us
    reshape x4, local copies, waits for them, and re-layouts, fold(): blocks.reshape(parts, n, 4, r // 4, w).transpose(0, 1, 3, 2, 4)  52.4 us
    reshape x8, local copies, waits for them, and re-layouts, unit_of(): return grad.astype(BF).reshape(dp, rows // dp, sections, cols // sections...  44.6 us
    squeeze x50, local copies, waits for them, and re-layouts, pick(): return lax.dynamic_index_in_dim(value, index, axis, keepdims=False)  26.5 us
    dot_general x10, matrix products, mm(): return jnp.dot(left, right, preferred_element_type=F32)  25.8 us
    dot_general x10, matrix products, mm_tn(): lax.dot_general(left, right, (((0,), (0,)), ((), ())), preferred_element_...  24.3 us
  transfers between devices with their start and end apart: 110, of which 44 were waited for; matrix products, arithmetic and copies ran while one was open for 44% of the time, Pallas kernels for 0%

profile of v1, /device:TPU:0, one launch (start us, length us, event | category | flops | bytes accessed | tf_op | source)
XLA Modules:
  0.0 992.6 jit_solution(18412296344292155750)
XLA Ops:
  44.6 10.3 %convert_bitcast_fusion = bf16[12,257,384]{2,1,0:T(8,128)(2,1)} fusion(bf16[12,257,1408]{2,1,0:T(8,128)(2,1)} %param.18, bf16[1408,192]{1,0:T(8,128)(2,1)S(1)} %get-tuple-element.39, bf16[1408,192]{1,0:T(8,128)(2,1)S(1)} %get-tuple-element.38), kind=kOutput, calls=%fused_computation.82 | convolution fusion | flops 3338211840 | bytes 12134400 | tf_op jit(solution)/shard_map/npf,fc->npc/dot_general | solution.py:270
  61.0 10.9 %copy.174 = bf16[32,257,384]{1,2,0:T(8,128)(2,1)} copy(bf16[32,257,384]{2,1,0:T(8,128)(2,1)} %gather_fusion) | data formatting | bytes 12632064 | tf_op jit(solution)/shard_map/jit(_take)/gather | solution.py:281
  72.0 8.5 copy_select_fusion
  253.4 12.4 %reshape.640 = bf16[4,8,4,96,192]{3,2,1,4,0:T(4,128)(2,1)} reshape(bf16[4,8,384,192]{2,1,3,0:T(8,128)(2,1)} %bitcast.1041) | data formatting | bytes 9437184 | tf_op jit(solution)/shard_map/reshape | solution.py:308
  265.8 13.8 %copy.223 = bf16[4,8,4,96,192]{4,2,3,1,0:T(4,128)(2,1)} copy(bf16[4,8,4,96,192]{3,2,1,4,0:T(4,128)(2,1)} %reshape.640) | data formatting | bytes 9437184 | tf_op jit(solution)/shard_map/reshape | solution.py:308
  279.6 11.6 %reshape_reshape.11 = bf16[4,4,2,96,768]{4,3,2,1,0:T(8,128)(2,1)} reshape(bf16[4,8,96,4,192]{4,3,2,1,0:T(4,128)(2,1)} %bitcast.1025) | data formatting | bytes 9437184 | tf_op jit(solution)/shard_map/reshape;reshape | solution.py:119
  299.0 9.7 reshape.636
  353.1 12.4 %reshape.630 = bf16[4,8,4,96,192]{3,2,1,4,0:T(4,128)(2,1)} reshape(bf16[4,8,384,192]{2,1,3,0:T(8,128)(2,1)} %bitcast.1042) | data formatting | bytes 9437184 | tf_op jit(solution)/shard_map/reshape | solution.py:308
  365.5 13.8 %copy.217 = bf16[4,8,4,96,192]{4,2,3,1,0:T(4,128)(2,1)} copy(bf16[4,8,4,96,192]{3,2,1,4,0:T(4,128)(2,1)} %reshape.630) | data formatting | bytes 9437184 | tf_op jit(solution)/shard_map/reshape | solution.py:308
  379.3 11.6 %reshape_reshape.10 = bf16[4,4,2,96,768]{4,3,2,1,0:T(8,128)(2,1)} reshape(bf16[4,8,96,4,192]{4,3,2,1,0:T(4,128)(2,1)} %bitcast.1026) | data formatting | bytes 9437184 | tf_op jit(solution)/shard_map/reshape;reshape | solution.py:119
  394.2 9.9 reshape.626
  432.6 7.5 convolution_bitcast_fusion
  440.2 23.7 %multiply_reduce_fusion = (f32[3]{0:T(128)S(1)}, f32[32,3,32,257]{3,2,1,0:T(8,128)S(1)}) fusion(f32[32,3,32,257]{3,2,1,0:T(8,128)S(1)} %bitcast.1034, f32[32,3,32,257]{3,2,1,0:T(8,128)} %fusion.13, f32[32,3,32,257]{3,2,1,0:T(8,128)} %copy-done.24, f32[32,3,32]{2,1,0:T(4,128)S(1)} %copy-done.55), kind=kOutput, calls=%fused_computation.42 | output fusion | flops 5529853 | bytes 12644364 | tf_op jit(solution)/shard_map/sub | solution.py:339
  473.6 6.9 copy.207
  480.5 16.9 %copy.208 = f32[32,257,384]{2,0,1:T(8,128)} copy(f32[32,257,384]{1,2,0:T(8,128)} %bitcast.1019) | data formatting | bytes 25264128 | tf_op jit(solution)/shard_map/reshape | solution.py:344
  497.4 8.2 convolution_convert_fusion.10
  505.7 8.7 fusion.39
  572.3 9.3 reshape.616
  583.1 7.3 pad_maximum_fusion.1
  642.1 14.2 %collective-permute-start.45 = (bf16[176,384]{1,0:T(8,128)(2,1)S(1)}, bf16[176,384]{1,0:T(8,128)(2,1)S(1)}, u32[]{:S(2)}, u32[]{:S(2)}) collective-permute-start(bf16[176,384]{1,0:T(8,128)(2,1)S(1)} %get-tuple-element.125), channel_id=1, source_target_pairs={{0,2},{1,3},{2,4},{3,5},{4,6},{5,7},{8,10},{9,11},{10,12},{11,13},... | collective-permute-start | bytes 405512 | tf_op jit(solution)/shard_map/ppermute | solution.py:104
  680.2 7.3 collective-permute-done.32
  734.0 9.7 collective-permute-start.38
  831.1 17.2 %collective-permute-done.98 = bf16[4,48,768]{2,1,0:T(8,128)(2,1)S(1)} collective-permute-done((bf16[4,48,768]{2,1,0:T(8,128)(2,1)S(1)}, bf16[4,48,768]{2,1,0:T(8,128)(2,1)S(1)}, u32[]{:S(2)}, u32[]{:S(2)}) %collective-permute-start.98) | collective-permute-done | bytes 294944 | tf_op jit(solution)/shard_map/ppermute | solution.py:55
  892.4 7.7 collective-permute-start.90
  (853 shorter events, 718.0 us)
Async XLA Ops:
  33.4 49.5 %collective-permute-start = (bf16[256,192]{0,1:T(8,128)(2,1)}, bf16[256,192]{0,1:T(8,128)(2,1)}, u32[]{:S(2)}, u32[]{:S(2)}) collective-permute-start(bf16[256,192]{0,1:T(8,128)(2,1)} %get-tuple-element.149), channel_id=1, source_target_pairs={{0,8},{8,0},{16,24},{24,16},{1,9},{9,1},{17,25},{25,17},{2,10},{10... | collective-permute-start | bytes 294920 | tf_op jit(solution)/shard_map/ppermute | solution.py:55
  36.4 48.1 %collective-permute-start.1 = (bf16[256,192]{0,1:T(8,128)(2,1)}, bf16[256,192]{0,1:T(8,128)(2,1)}, u32[]{:S(2)}, u32[]{:S(2)}) collective-permute-start(bf16[256,192]{0,1:T(8,128)(2,1)} %get-tuple-element.148), channel_id=1, source_target_pairs={{0,16},{8,24},{16,0},{24,8},{1,17},{9,25},{17,1},{25,9},{2,18},{10... | collective-permute-start | bytes 294920 | tf_op jit(solution)/shard_map/ppermute | solution.py:55
  37.9 48.1 %collective-permute-start.2 = (bf16[256,192]{0,1:T(8,128)(2,1)}, bf16[256,192]{0,1:T(8,128)(2,1)}, u32[]{:S(2)}, u32[]{:S(2)}) collective-permute-start(bf16[256,192]{0,1:T(8,128)(2,1)} %get-tuple-element.147), channel_id=1, source_target_pairs={{0,24},{8,16},{16,8},{24,0},{1,25},{9,17},{17,9},{25,1},{2,26},{10... | collective-permute-start | bytes 294920 | tf_op jit(solution)/shard_map/ppermute | solution.py:55
  235.3 179.3 %collective-permute-start.9 = (bf16[256,192]{0,1:T(8,128)(2,1)}, bf16[256,192]{0,1:T(8,128)(2,1)}, u32[]{:S(2)}, u32[]{:S(2)}) collective-permute-start(bf16[256,192]{0,1:T(8,128)(2,1)} %get-tuple-element.143), channel_id=1, source_target_pairs={{0,8},{8,0},{16,24},{24,16},{1,9},{9,1},{17,25},{25,17},{2,10},{10... | collective-permute-start | bytes 294920 | tf_op jit(solution)/shard_map/ppermute | solution.py:55
  236.6 184.6 %collective-permute-start.10 = (bf16[256,192]{0,1:T(8,128)(2,1)}, bf16[256,192]{0,1:T(8,128)(2,1)}, u32[]{:S(2)}, u32[]{:S(2)}) collective-permute-start(bf16[256,192]{0,1:T(8,128)(2,1)} %get-tuple-element.142), channel_id=1, source_target_pairs={{0,16},{8,24},{16,0},{24,8},{1,17},{9,25},{17,1},{25,9},{2,18},{10... | collective-permute-start | bytes 294920 | tf_op jit(solution)/shard_map/ppermute | solution.py:55
  237.2 186.9 %collective-permute-start.11 = (bf16[256,192]{0,1:T(8,128)(2,1)}, bf16[256,192]{0,1:T(8,128)(2,1)}, u32[]{:S(2)}, u32[]{:S(2)}) collective-permute-start(bf16[256,192]{0,1:T(8,128)(2,1)} %get-tuple-element.141), channel_id=1, source_target_pairs={{0,24},{8,16},{16,8},{24,0},{1,25},{9,17},{17,9},{25,1},{2,26},{10... | collective-permute-start | bytes 294920 | tf_op jit(solution)/shard_map/ppermute | solution.py:55
  294.5 458.6 %collective-permute-start.94 = (bf16[4,4,96,768]{3,2,1,0:T(8,128)(2,1)}, bf16[4,4,96,768]{3,2,1,0:T(8,128)(2,1)}, u32[]{:S(2)}, u32[]{:S(2)}) collective-permute-start(bf16[4,4,96,768]{3,2,1,0:T(8,128)(2,1)} %dynamic-slice_bitcast_fusion), channel_id=1, source_target_pairs={{0,1},{1,0},{2,3},{3,2},{4,5},{5,4},{6,7},{7,6},{8,9},{9,8},{10,11... | collective-permute-start | bytes 7077896 | tf_op jit(solution)/shard_map/ppermute | solution.py:55
  315.9 446.6 %collective-permute-start.83 = (bf16[4,4,96,768]{3,2,1,0:T(8,128)(2,1)}, bf16[4,4,96,768]{3,2,1,0:T(8,128)(2,1)}, u32[]{:S(2)}, u32[]{:S(2)}) collective-permute-start(bf16[4,4,96,768]{3,2,1,0:T(8,128)(2,1)} %bitcast.1016), channel_id=1, source_target_pairs={{0,1},{1,0},{2,3},{3,2},{4,5},{5,4},{6,7},{7,6},{8,9},{9,8},{10,11... | collective-permute-start | bytes 7077896 | tf_op jit(solution)/shard_map/ppermute | solution.py:55
  414.6 342.4 %collective-permute-start.72 = (bf16[4,4,96,768]{3,0,2,1:T(4,128)(2,1)}, bf16[4,4,96,768]{3,0,2,1:T(4,128)(2,1)}, u32[]{:S(2)}, u32[]{:S(2)}) collective-permute-start(bf16[4,4,96,768]{3,0,2,1:T(4,128)(2,1)} %dynamic-slice_bitcast_fusion.1), channel_id=1, source_target_pairs={{0,1},{1,0},{2,3},{3,2},{4,5},{5,4},{6,7},{7,6},{8,9},{9,8},{10,11... | collective-permute-start | bytes 7077896 | tf_op jit(solution)/shard_map/ppermute | solution.py:55
  421.2 97.8 %collective-permute-start.6 = (bf16[256,192]{0,1:T(8,128)(2,1)}, bf16[256,192]{0,1:T(8,128)(2,1)S(1)}, u32[]{:S(2)}, u32[]{:S(2)}) collective-permute-start(bf16[256,192]{0,1:T(8,128)(2,1)} %get-tuple-element.146), channel_id=1, source_target_pairs={{0,8},{8,0},{16,24},{24,16},{1,9},{9,1},{17,25},{25,17},{2,10},{10... | collective-permute-start | bytes 294920 | tf_op jit(solution)/shard_map/ppermute | solution.py:55
  424.1 95.7 %collective-permute-start.7 = (bf16[256,192]{0,1:T(8,128)(2,1)}, bf16[256,192]{0,1:T(8,128)(2,1)S(1)}, u32[]{:S(2)}, u32[]{:S(2)}) collective-permute-start(bf16[256,192]{0,1:T(8,128)(2,1)} %get-tuple-element.145), channel_id=1, source_target_pairs={{0,16},{8,24},{16,0},{24,8},{1,17},{9,25},{17,1},{25,9},{2,18},{10... | collective-permute-start | bytes 294920 | tf_op jit(solution)/shard_map/ppermute | solution.py:55
  526.3 82.4 %collective-permute-start.40 = (bf16[1,4,176,384]{3,2,1,0:T(8,128)(2,1)}, bf16[1,4,176,384]{3,2,1,0:T(8,128)(2,1)}, u32[]{:S(2)}, u32[]{:S(2)}) collective-permute-start(bf16[1,4,176,384]{3,2,1,0:T(8,128)(2,1)} %dynamic-slice_bitcast_fusion.17), channel_id=1, source_target_pairs={{0,1},{1,0},{2,3},{3,2},{4,5},{5,4},{6,7},{7,6},{8,9},{9,8},{10,11... | collective-permute-start | bytes 1622024 | tf_op jit(solution)/shard_map/ppermute | solution.py:55
  629.9 46.0 %collective-permute-start.29 = (bf16[4,4,96,384]{3,0,2,1:T(4,128)(2,1)}, bf16[4,4,96,384]{3,0,2,1:T(4,128)(2,1)}, u32[]{:S(2)}, u32[]{:S(2)}) collective-permute-start(bf16[4,4,96,384]{3,0,2,1:T(4,128)(2,1)} %dynamic-slice_bitcast_fusion.4), channel_id=1, source_target_pairs={{0,1},{1,0},{2,3},{3,2},{4,5},{5,4},{6,7},{7,6},{8,9},{9,8},{10,11... | collective-permute-start | bytes 3538952 | tf_op jit(solution)/shard_map/ppermute | solution.py:55
  672.1 95.0 %collective-permute-start.61 = (bf16[4,4,96,768]{3,2,1,0:T(8,128)(2,1)}, bf16[4,4,96,768]{3,2,1,0:T(8,128)(2,1)}, u32[]{:S(2)}, u32[]{:S(2)}) collective-permute-start(bf16[4,4,96,768]{3,2,1,0:T(8,128)(2,1)} %dynamic-slice_bitcast_fusion.2), channel_id=1, source_target_pairs={{0,1},{1,0},{2,3},{3,2},{4,5},{5,4},{6,7},{7,6},{8,9},{9,8},{10,11... | collective-permute-start | bytes 7077896 | tf_op jit(solution)/shard_map/ppermute | solution.py:55
  772.9 25.6 %collective-permute-start.75 = (bf16[2,4,48,768]{3,2,1,0:T(8,128)(2,1)S(1)}, bf16[2,4,48,768]{3,2,1,0:T(8,128)(2,1)S(1)}, u32[]{:S(2)}, u32[]{:S(2)}) collective-permute-start(bf16[2,4,48,768]{3,2,1,0:T(8,128)(2,1)S(1)} %dynamic-slice_bitcast_fusion.9), channel_id=1, source_target_pairs={{0,16},{8,24},{16,0},{24,8},{1,17},{9,25},{17,1},{25,9},{2,18},{10... | collective-permute-start | bytes 1769480 | tf_op jit(solution)/shard_map/ppermute | solution.py:55
  776.3 27.8 %collective-permute-start.73 = (bf16[2,4,48,768]{3,2,1,0:T(8,128)(2,1)S(1)}, bf16[2,4,48,768]{3,2,1,0:T(8,128)(2,1)S(1)}, u32[]{:S(2)}, u32[]{:S(2)}) collective-permute-start(bf16[2,4,48,768]{3,2,1,0:T(8,128)(2,1)S(1)} %dynamic-slice_bitcast_fusion.10), channel_id=1, source_target_pairs={{0,8},{8,0},{16,24},{24,16},{1,9},{9,1},{17,25},{25,17},{2,10},{10... | collective-permute-start | bytes 1769480 | tf_op jit(solution)/shard_map/ppermute | solution.py:55
  778.8 32.3 %collective-permute-start.64 = (bf16[2,4,48,768]{3,2,1,0:T(8,128)(2,1)S(1)}, bf16[2,4,48,768]{3,2,1,0:T(8,128)(2,1)S(1)}, u32[]{:S(2)}, u32[]{:S(2)}) collective-permute-start(bf16[2,4,48,768]{3,2,1,0:T(8,128)(2,1)S(1)} %dynamic-slice_bitcast_fusion.11), channel_id=1, source_target_pairs={{0,16},{8,24},{16,0},{24,8},{1,17},{9,25},{17,1},{25,9},{2,18},{10... | collective-permute-start | bytes 1769480 | tf_op jit(solution)/shard_map/ppermute | solution.py:55
  785.9 30.9 %collective-permute-start.62 = (bf16[2,4,48,768]{3,2,1,0:T(8,128)(2,1)S(1)}, bf16[2,4,48,768]{3,2,1,0:T(8,128)(2,1)S(1)}, u32[]{:S(2)}, u32[]{:S(2)}) collective-permute-start(bf16[2,4,48,768]{3,2,1,0:T(8,128)(2,1)S(1)} %dynamic-slice_bitcast_fusion.12), channel_id=1, source_target_pairs={{0,8},{8,0},{16,24},{24,16},{1,9},{9,1},{17,25},{25,17},{2,10},{10... | collective-permute-start | bytes 1769480 | tf_op jit(solution)/shard_map/ppermute | solution.py:55
  791.5 32.3 %collective-permute-start.53 = (bf16[2,4,48,768]{3,2,1,0:T(8,128)(2,1)S(1)}, bf16[2,4,48,768]{3,2,1,0:T(8,128)(2,1)S(1)}, u32[]{:S(2)}, u32[]{:S(2)}) collective-permute-start(bf16[2,4,48,768]{3,2,1,0:T(8,128)(2,1)S(1)} %dynamic-slice_bitcast_fusion.13), channel_id=1, source_target_pairs={{0,16},{8,24},{16,0},{24,8},{1,17},{9,25},{17,1},{25,9},{2,18},{10... | collective-permute-start | bytes 1769480 | tf_op jit(solution)/shard_map/ppermute | solution.py:55
  798.5 30.9 %collective-permute-start.51 = (bf16[2,4,48,768]{3,2,1,0:T(8,128)(2,1)S(1)}, bf16[2,4,48,768]{3,2,1,0:T(8,128)(2,1)S(1)}, u32[]{:S(2)}, u32[]{:S(2)}) collective-permute-start(bf16[2,4,48,768]{3,2,1,0:T(8,128)(2,1)S(1)} %dynamic-slice_bitcast_fusion.14), channel_id=1, source_target_pairs={{0,8},{8,0},{16,24},{24,16},{1,9},{9,1},{17,25},{25,17},{2,10},{10... | collective-permute-start | bytes 1769480 | tf_op jit(solution)/shard_map/ppermute | solution.py:55
  804.1 67.9 %collective-permute-start.21 = (bf16[2,4,48,768]{3,2,1,0:T(8,128)(2,1)S(1)}, bf16[2,4,48,768]{3,2,1,0:T(8,128)(2,1)S(1)}, u32[]{:S(2)}, u32[]{:S(2)}) collective-permute-start(bf16[2,4,48,768]{3,2,1,0:T(8,128)(2,1)S(1)} %dynamic-slice_bitcast_fusion.15), channel_id=1, source_target_pairs={{0,16},{8,24},{16,0},{24,8},{1,17},{9,25},{17,1},{25,9},{2,18},{10... | collective-permute-start | bytes 1769480 | tf_op jit(solution)/shard_map/ppermute | solution.py:55
  811.2 67.1 %collective-permute-start.19 = (bf16[2,4,48,768]{3,2,1,0:T(8,128)(2,1)S(1)}, bf16[2,4,48,768]{3,2,1,0:T(8,128)(2,1)S(1)}, u32[]{:S(2)}, u32[]{:S(2)}) collective-permute-start(bf16[2,4,48,768]{3,2,1,0:T(8,128)(2,1)S(1)} %dynamic-slice_bitcast_fusion.16), channel_id=1, source_target_pairs={{0,8},{8,0},{16,24},{24,16},{1,9},{9,1},{17,25},{25,17},{2,10},{10... | collective-permute-start | bytes 1769480 | tf_op jit(solution)/shard_map/ppermute | solution.py:55
  816.8 31.6 %collective-permute-start.98 = (bf16[4,48,768]{2,1,0:T(8,128)(2,1)S(1)}, bf16[4,48,768]{2,1,0:T(8,128)(2,1)S(1)}, u32[]{:S(2)}, u32[]{:S(2)}) collective-permute-start(bf16[4,48,768]{2,1,0:T(8,128)(2,1)S(1)} %dynamic-slice_bitcast_fusion.18), channel_id=1, source_target_pairs={{0,8},{8,0},{16,24},{24,16},{1,9},{9,1},{17,25},{25,17},{2,10},{10... | collective-permute-start | bytes 884744 | tf_op jit(solution)/shard_map/ppermute | solution.py:55
  829.4 25.3 %collective-permute-start.87 = (bf16[4,48,768]{2,1,0:T(8,128)(2,1)S(1)}, bf16[4,48,768]{2,1,0:T(8,128)(2,1)S(1)}, u32[]{:S(2)}, u32[]{:S(2)}) collective-permute-start(bf16[4,48,768]{2,1,0:T(8,128)(2,1)S(1)} %dynamic-slice_bitcast_fusion.20), channel_id=1, source_target_pairs={{0,8},{8,0},{16,24},{24,16},{1,9},{9,1},{17,25},{25,17},{2,10},{10... | collective-permute-start | bytes 884744 | tf_op jit(solution)/shard_map/ppermute | solution.py:55
  (203 other events, 1801.6 us)
